TPU v7x, 32 devices: a whole 2x2x4 slice. The times are simulated.
32 devices in a mesh: grp: 2 (over x), lat: 8 (over z, y), row: 2 (over core).
Axes of the slice: x: 2, y: 2, z: 4, core: 2. Of those that a mesh axis runs over, the one named last changes fastest.
Arguments:
- activations: bfloat16 [2560, 4096], P(('grp', 'row')), parts along dimension 0, may hold values from -6 to 6
- enc_weight: float32 [8192, 8192], P(('grp', 'row'), 'lat'), parts along dimension 0, may hold values from -0.09375 to 0.09375
- dec_weight: float32 [16384, 4096], P(('grp', 'lat'), 'row'), parts along dimension 0, may hold values from -0.0625 to 0.0625
- enc_bias: float32 [16384], P(('grp', 'lat')), parts along dimension 0, may hold values from -3 to 3
- dec_bias: float32 [8192], P('grp'), parts along dimension 0, may hold values from -3 to 3
- enc_first: bfloat16 [8192, 8192], P(('grp', 'row'), 'lat'), parts along dimension 0, may hold values from -0.125 to 0.125
- enc_second: bfloat16 [8192, 8192], P(('grp', 'row'), 'lat'), parts along dimension 0, may hold values from 1.9520521e-06 to 0.00019454956
- dec_first: bfloat16 [16384, 4096], P(('grp', 'lat'), 'row'), parts along dimension 0, may hold values from -0.125 to 0.125
- dec_second: bfloat16 [16384, 4096], P(('grp', 'lat'), 'row'), parts along dimension 0, may hold values from 1.9520521e-06 to 0.00019454956
Outputs:
- enc_step: bfloat16 [8192, 8192], P(('grp', 'row'), 'lat'), parts along dimension 0
- dec_step: bfloat16 [16384, 4096], P(('grp', 'lat'), 'row'), parts along dimension 0
There are 2 independent parts, one for each index of `grp`. A program takes and returns all parts, laid end to end along the dimension named above; each array names one. Nothing has to cross between parts.
All inputs are finite; a program needn't handle non-finite values.
Results may differ from a plain program's by a relative error of at most 0.012.
The roundings to bfloat16 on the way count: a program that leaves them out, or rounds other values in their place, can miss the bound.
Values may be sent and summed in bfloat16 or wider, within the bound.
A program may use at most 192 MiB of HBM per device.

v0:
```python
import jax
import jax.numpy as jnp
from jax import lax
from jax.sharding import PartitionSpec as P

l1_weight = 0.8
beta_one = 0.9
beta_two = 0.999
adam_eps = 1e-08
step_count = 1000.0


def adam_step(gradient, first, second):
    moment_one = beta_one * first.astype(jnp.float32) + (1.0 - beta_one) * gradient
    moment_two = beta_two * second.astype(jnp.float32) + (1.0 - beta_two) * gradient * gradient
    scaled_one = moment_one / (1.0 - beta_one**step_count)
    scaled_two = moment_two / (1.0 - beta_two**step_count)
    return (scaled_one / (jnp.sqrt(scaled_two) + adam_eps)).astype(jnp.bfloat16)


def rows_product(left_rows, right_rows):
    return lax.dot_general(
        left_rows, right_rows, (((0,), (0,)), ((), ())), preferred_element_type=jnp.float32
    )


def on_device(
    activations,
    enc_weight,
    dec_weight,
    enc_bias,
    dec_bias,
    enc_first,
    enc_second,
    dec_first,
    dec_second,
):
    local_rows = activations.shape[0]
    total_rows = local_rows * lax.axis_size("row")
    acts_full = activations.astype(jnp.float32)
    centered = (acts_full - dec_bias).astype(jnp.bfloat16)
    enc_low = enc_weight.astype(jnp.bfloat16)
    dec_low = dec_weight.astype(jnp.bfloat16)
    col_block = centered
    preact = (
        jnp.dot(
            col_block,
            lax.all_gather(enc_low, "row", axis=0, tiled=True),
            preferred_element_type=jnp.float32,
        )
        + enc_bias
    )
    latent_codes = jnp.maximum(preact, 0.0).astype(jnp.bfloat16)
    dec_full = lax.all_gather(dec_low, "row", axis=1, tiled=True)
    partial_recon = jnp.dot(latent_codes, dec_full, preferred_element_type=jnp.float32)
    recon = lax.psum(partial_recon, "lat") + dec_bias
    residual_grad = (2.0 / total_rows * (recon - acts_full)).astype(jnp.bfloat16)
    code_grad = (
        jnp.einsum("rd,ld->rl", residual_grad, dec_full, preferred_element_type=jnp.float32)
        + l1_weight / total_rows
    )
    pre_grad = jnp.where(preact > 0, code_grad, 0.0).astype(jnp.bfloat16)
    grad_dec = lax.psum_scatter(
        rows_product(latent_codes, residual_grad).astype(jnp.bfloat16),
        "row",
        scatter_dimension=1,
        tiled=True,
    ).astype(jnp.float32)
    col_block = centered
    grad_enc = lax.psum_scatter(
        rows_product(col_block, pre_grad), "row", scatter_dimension=0, tiled=True
    )
    return (adam_step(grad_enc, enc_first, enc_second), adam_step(grad_dec, dec_first, dec_second))


def solution(mesh):
    return jax.shard_map(
        on_device,
        mesh=mesh,
        in_specs=(
            P(("grp", "row"), None),
            P(("grp", "row"), "lat"),
            P(("grp", "lat"), "row"),
            P(("grp", "lat")),
            P("grp"),
            P(("grp", "row"), "lat"),
            P(("grp", "row"), "lat"),
            P(("grp", "lat"), "row"),
            P(("grp", "lat"), "row"),
        ),
        out_specs=(P(("grp", "row"), "lat"), P(("grp", "lat"), "row")),
        check_vma=False,
    )
```

profile of v0, /device:TPU:0, one launch (start us, length us, event | category | flops | bytes accessed | tf_op | source)
XLA Modules:
  0.0 484.2 jit_solution(7781758373667180796)
XLA Ops:
  7.2 0.0 all-gather.3.cloned.1.call-start
  7.2 6.1 %convert_element_type.48 = bf16[2048,1024]{1,0:T(8,128)(2,1)} convert(f32[2048,1024]{1,0:T(8,128)} %param.10) | non-fusion elementwise | flops 2097152 | bytes 12582912 | tf_op jit(solution)/shard_map/convert_element_type | solution.py:42
  13.3 0.0 all-gather.3.cloned.1.call-update
  13.3 0.0 copy-start.1
  13.3 0.0 all-gather.5.cloned.1.call-start
  13.4 6.1 %convert_element_type.50 = bf16[1024,2048]{1,0:T(8,128)(2,1)} convert(f32[1024,2048]{1,0:T(8,128)} %param.11) | non-fusion elementwise | flops 2097152 | bytes 12582912 | tf_op jit(solution)/shard_map/convert_element_type | solution.py:43
  19.4 0.0 all-gather.5.cloned.1.call-update
  19.4 0.0 copy-start
  19.4 0.0 all-reduce.2.cloned.1.call-start
  19.5 16.5 %all-gather.3.cloned.1.call-done = bf16[4096,1024]{1,0:T(8,128)(2,1)} async-done(((bf16[2048,1024]{1,0:T(8,128)(2,1)}), bf16[4096,1024]{1,0:T(8,128)(2,1)}) %all-gather.3.cloned.1.call-update) | async-done | bytes 8388624 | tf_op jit(solution)/shard_map/all_gather | solution.py:48
  36.0 0.0 copy-done.1
  36.0 9.5 %fusion.18 = f32[640,1024]{1,0:T(8,128)S(1)} fusion(bf16[4096,1024]{1,0:T(8,128)(2,1)} %all-gather.3.cloned.1.call-done, bf16[640,4096]{1,0:T(8,128)(2,1)} %param.9, f32[4096]{0:T(1024)S(1)} %copy-done.1), kind=kOutput, calls=%fused_computation.23 | convolution fusion | flops 5376573440 | bytes 16269312 | tf_op jit(solution)/shard_map/dot_general | solution.py:46
  45.6 13.6 %all-gather.5.cloned.1.call-done = bf16[1024,4096]{1,0:T(8,128)(2,1)} async-done(((bf16[1024,2048]{1,0:T(8,128)(2,1)}), bf16[1024,4096]{1,0:T(8,128)(2,1)}) %all-gather.5.cloned.1.call-update) | async-done | bytes 8388624 | tf_op jit(solution)/shard_map/all_gather | solution.py:54
  59.2 0.0 copy-done
  59.2 11.5 %fusion.21 = f32[640,4096]{1,0:T(8,128)} fusion(bf16[1024,4096]{1,0:T(8,128)(2,1)} %all-gather.5.cloned.1.call-done, f32[640,1024]{1,0:T(8,128)S(1)} %fusion.18, f32[1024]{0:T(1024)S(1)} %copy-done), kind=kOutput, calls=%fused_computation.27 | convolution fusion | flops 5370675200 | bytes 21499904 | tf_op jit(solution)/shard_map/dot_general | solution.py:55
  70.7 0.0 all-reduce.2.cloned.1.call-update
  70.7 0.0 reduce-scatter.5.cloned.1.call-start
  70.7 328.7 %all-reduce.2.cloned.1.call-done = f32[640,4096]{1,0:T(8,128)} async-done(((f32[640,4096]{1,0:T(8,128)}), f32[640,4096]{1,0:T(8,128)}) %all-reduce.2.cloned.1.call-update) | async-done | bytes 10485776 | tf_op jit(solution)/shard_map/psum | solution.py:56
  399.4 14.8 %convolution_convert_fusion = bf16[1024,4096]{1,0:T(8,128)(2,1)} fusion(f32[640,1024]{1,0:T(8,128)S(1)} %fusion.18, f32[1024]{0:T(1024)S(1)} %copy-done, bf16[640,4096]{1,0:T(8,128)(2,1)} %param.9, f32[640,4096]{1,0:T(8,128)} %all-reduce.2.cloned.1.call-done, f32[4096]{0:T(1024)S(1)} %copy-done.1), kind=kOutput, calls=%fused_computation.21 | convolution fusion | flops 5387976704 | bytes 26759168 | tf_op jit(solution)/shard_map/dot_general | solution.py:22
  414.2 0.0 reduce-scatter.5.cloned.1.call-update
  414.2 0.2 reduce-scatter.3.cloned.1.call-start
  414.4 27.5 %fusion.16 = f32[4096,1024]{1,0:T(8,128)} fusion(bf16[640,4096]{1,0:T(8,128)(2,1)} %param.9, f32[4096]{0:T(1024)S(1)} %copy-done.1, f32[640,1024]{1,0:T(8,128)S(1)} %fusion.18, bf16[1024,4096]{1,0:T(8,128)(2,1)} %all-gather.5.cloned.1.call-done, f32[1024]{0:T(1024)S(1)} %copy-done, f32[640,4096]{1,0:T(8,128)} %all-reduce.2.cloned.1.call-done), kind=kOutput, calls=%fused_computation.22 | convolution fusion | flops 10761666560 | bytes 43536384 | tf_op jit(solution)/shard_map/dot_general | solution.py:22
  441.9 0.0 reduce-scatter.3.cloned.1.call-update
  441.9 0.0 reduce-scatter.5.cloned.1.call-done
  442.0 10.3 %fusion.5 = bf16[1024,2048]{1,0:T(8,128)(2,1)} fusion(bf16[1024,2048]{1,0:T(8,128)(2,1)} %reduce-scatter.5.cloned.1.call-done, bf16[1024,2048]{1,0:T(8,128)(2,1)} %param.17, bf16[1024,2048]{1,0:T(8,128)(2,1)} %param.16), kind=kLoop, calls=%fused_computation.10 | loop fusion | flops 29360128 | bytes 16777216 | tf_op jit(solution)/shard_map/convert_element_type | solution.py:18
  452.2 14.6 %reduce-scatter.3.cloned.1.call-done = f32[2048,1024]{1,0:T(8,128)} async-done(((f32[4096,1024]{1,0:T(8,128)}), f32[2048,1024]{1,0:T(8,128)}) %reduce-scatter.3.cloned.1.call-update) | async-done | bytes 8388624 | tf_op jit(solution)/shard_map/reduce_scatter | solution.py:70
  466.9 10.8 %fusion.15 = bf16[2048,1024]{1,0:T(8,128)(2,1)} fusion(f32[2048,1024]{1,0:T(8,128)} %reduce-scatter.3.cloned.1.call-done, bf16[2048,1024]{1,0:T(8,128)(2,1)} %param.15, bf16[2048,1024]{1,0:T(8,128)(2,1)} %param.14), kind=kLoop, calls=%fused_computation.20 | loop fusion | flops 27262976 | bytes 20971520 | tf_op jit(solution)/shard_map/convert_element_type | solution.py:18
Async XLA Ops:
  7.2 28.8 %all-gather.3.cloned.1.call-start = ((), (), s32[]{:S(2)}) async-start(), calls=%async_computation.2 | async-start | bytes 12582912 | tf_op jit(solution)/shard_map/all_gather | solution.py:48
  13.3 22.7 %copy-start.1 = (f32[4096]{0:T(1024)S(1)}, f32[4096]{0:T(1024)}, u32[]{:S(2)}) copy-start(f32[4096]{0:T(1024)} %param.13) | copy-start | bytes 49156
  13.3 45.9 %all-gather.5.cloned.1.call-start = ((), (), s32[]{:S(2)}) async-start(), calls=%async_computation.3 | async-start | bytes 12582912 | tf_op jit(solution)/shard_map/all_gather | solution.py:54
  19.4 39.7 %copy-start = (f32[1024]{0:T(1024)S(1)}, f32[1024]{0:T(1024)}, u32[]{:S(2)}) copy-start(f32[1024]{0:T(1024)} %param.12) | copy-start | bytes 12292
  19.4 380.0 %all-reduce.2.cloned.1.call-start = ((), (), s32[]{:S(2)}) async-start(), calls=%async_computation.4 | async-start | bytes 20971520 | tf_op jit(solution)/shard_map/psum | solution.py:56
  70.7 371.3 %reduce-scatter.5.cloned.1.call-start = ((), (), s32[]{:S(2)}) async-start(), calls=%async_computation.6 | async-start | bytes 12582912 | tf_op jit(solution)/shard_map/reduce_scatter | solution.py:63
  414.2 52.7 %reduce-scatter.3.cloned.1.call-start = ((), (), s32[]{:S(2)}) async-start(), calls=%async_computation.5 | async-start | bytes 25165824 | tf_op jit(solution)/shard_map/reduce_scatter | solution.py:70
Sparse Core Ops, SparseCore 0:
  13.4 22.5 all-gather.2
  38.1 21.0 all-gather.4
  70.8 328.5 all-reduce.1
  414.3 15.8 reduce-scatter.4
  442.1 24.7 reduce-scatter.2
where the time goes:
time: 484 us
  waiting for transfers between devices  374 us (77%)
  matrix products  63.3 us (13%)
  other arithmetic  33.2 us (7%)
  between operations  13.8 us (3%)
    psum x1, waiting for transfers between devices, on_device(): recon = lax.psum(partial_recon, 'lat') + dec_bias  329 us
    dot_general x2, matrix products, rows_product(): lax.dot_general(left_rows, right_rows, (((0,), (0,)), ((), ())), preferre...  42.2 us
    convert_element_type x2, other arithmetic, adam_step(): return (scaled_one / (jnp.sqrt(scaled_two) + adam_eps)).astype(jnp.bfloat16)  21 us
    all_gather x1, waiting for transfers between devices, on_device(): lax.all_gather(enc_low, 'row', axis=0, tiled=True)  16.5 us
    reduce_scatter x1, waiting for transfers between devices, on_device(): lax.psum_scatter(rows_product(col_block, pre_grad), 'row', scatter_dimens...  14.6 us
    all_gather x1, waiting for transfers between devices, on_device(): dec_full = lax.all_gather(dec_low, 'row', axis=1, tiled=True)  13.6 us
    dot_general x1, matrix products, on_device(): jnp.dot(latent_codes, dec_full, preferred_element_type=jnp.float32)  11.5 us
  transfers between devices with their start and end apart: 5, of which 4 were waited for; matrix products, arithmetic and copies ran while one was open for 11% of the time, Pallas kernels for 0%

commit v1 on v0

v1 whole, which is shorter than its diff:
```python
import functools

import jax
import jax.numpy as jnp
from jax import lax
from jax.experimental import pallas as pl
from jax.experimental.pallas import tpu as pltpu
from jax.sharding import PartitionSpec as P

l1_weight = 0.8
beta_one = 0.9
beta_two = 0.999
adam_eps = 1e-08
step_count = 1000.0
subs = 4


def adam_step(gradient, first, second):
    moment_one = beta_one * first.astype(jnp.float32) + (1.0 - beta_one) * gradient
    moment_two = beta_two * second.astype(jnp.float32) + (1.0 - beta_two) * gradient * gradient
    scaled_one = moment_one / (1.0 - beta_one**step_count)
    scaled_two = moment_two / (1.0 - beta_two**step_count)
    return (scaled_one / (jnp.sqrt(scaled_two) + adam_eps)).astype(jnp.bfloat16)


def rows_product(left_rows, right_rows):
    return lax.dot_general(
        left_rows, right_rows, (((0,), (0,)), ((), ())), preferred_element_type=jnp.float32
    )


def ring_kernel(
    n,
    snake,
    total_rows,
    preact_ref,
    dec_own_ref,
    dec_peer_ref,
    bias_ref,
    acts_ref,
    pre_grad_ref,
    own_ref,
    recv_ref,
    dec,
    acts,
    sums,
    resid,
    codes,
    codes_t,
    code_grad,
    part,
    outgoing,
    rs_send,
    rs_recv,
    ag_send,
    ag_recv,
    x_send,
    x_recv,
    load_sem,
):
    rows, lats = preact_ref.shape
    width = resid.shape[2]
    half = n // 2
    sub_rows = rows // subs
    half_rows = rows // 2
    pieces = max(1, min(subs, lats // 256))
    piece = lats // pieces
    me = lax.axis_index("lat")
    row = lax.axis_index("row")

    def lat_of(pos):
        if not snake:
            return pos
        return jnp.where(pos < half, 2 * pos, 2 * (n - 1 - pos) + 1)

    if snake:
        pos = jnp.where(lax.rem(me, 2) == 0, me // 2, n - 1 - me // 2)
    else:
        pos = me
    targets = (lat_of(lax.rem(pos + 1, n)), lat_of(lax.rem(pos + n - 1, n)))

    barrier = pltpu.get_barrier_semaphore()
    for target in targets:
        pl.semaphore_signal(
            barrier, inc=1, device_id={"lat": target}, device_id_type=pl.DeviceIdType.MESH
        )
    pl.semaphore_signal(
        barrier, inc=1, device_id={"row": 1 - row}, device_id_type=pl.DeviceIdType.MESH
    )

    def shard_at(offset):
        return lax.rem(pos + offset + 2 * n, n)

    def columns(shard):
        return pl.ds(pl.multiple_of(lax.rem(shard, half) * width, width), width)

    load_own = pltpu.make_async_copy(dec_own_ref, dec.at[row], load_sem.at[0])
    load_peer = pltpu.make_async_copy(dec_peer_ref, dec.at[1 - row], load_sem.at[1])
    wide = pl.ds(pl.multiple_of(pos * width, width), width)
    load_acts = pltpu.make_async_copy(acts_ref.at[:, wide], acts, load_sem.at[2])
    load_own.start()
    load_peer.start()
    load_acts.start()
    codes[...] = jnp.maximum(preact_ref[...], 0.0).astype(jnp.bfloat16)
    load_own.wait()
    load_peer.wait()
    pl.semaphore_wait(barrier, 3)

    def dec_block(shard, lat_slice=slice(None)):
        return dec[shard // half, lat_slice, columns(shard)]

    def partial(way, shard):
        return jnp.dot(
            codes[pl.ds(way * half_rows, half_rows), :],
            dec_block(shard),
            preferred_element_type=jnp.float32,
        )

    def rs_copy(step, chain):
        return pltpu.make_async_remote_copy(
            src_ref=sums.at[step, chain],
            dst_ref=sums.at[step + 1, chain],
            send_sem=rs_send.at[step, chain],
            recv_sem=rs_recv.at[step, chain],
            device_id={"lat": targets[chain // 2]},
            device_id_type=pl.DeviceIdType.MESH,
        )

    def ag_copy(way, step, sub):
        shard = shard_at(-step if way == 0 else step)
        block = resid.at[shard, pl.ds(sub * sub_rows, sub_rows), :]
        return pltpu.make_async_remote_copy(
            src_ref=block,
            dst_ref=block,
            send_sem=ag_send.at[way, step, sub],
            recv_sem=ag_recv.at[way, step, sub],
            device_id={"lat": targets[way]},
            device_id_type=pl.DeviceIdType.MESH,
        )

    def exchange(block):
        place = pl.ds(pl.multiple_of(block * width, width), width)
        return pltpu.make_async_remote_copy(
            src_ref=outgoing.at[block],
            dst_ref=recv_ref.at[:, place],
            send_sem=x_send.at[block],
            recv_sem=x_recv.at[block],
            device_id={"row": 1 - row},
            device_id_type=pl.DeviceIdType.MESH,
        )

    for way in range(2):
        first = partial(way, shard_at(-1 if way == 0 else 1))
        for sub in range(2):
            chain = way * 2 + sub
            sums[0, chain] = first[sub * sub_rows : (sub + 1) * sub_rows].astype(jnp.bfloat16)
            rs_copy(0, chain).start()
    codes_t[...] = jnp.maximum(jnp.transpose(preact_ref[...]), 0.0).astype(jnp.bfloat16)

    def own_term(way, sub):
        return part[way, pl.ds(sub * sub_rows, sub_rows), :]

    @pl.loop(1, n - 1)
    def _(step):
        for way in range(2):
            part[way] = partial(way, shard_at(-1 - step if way == 0 else 1 + step))
        for sub in range(2):
            for way in range(2):
                chain = way * 2 + sub
                rs_copy(step - 1, chain).wait_recv()
                sums[step, chain] = (
                    sums[step, chain].astype(jnp.float32) + own_term(way, sub)
                ).astype(jnp.bfloat16)
                rs_copy(step, chain).start()

    for way in range(2):
        part[way] = partial(way, pos)
    load_acts.wait()
    for sub in range(2):
        for way in range(2):
            chain = way * 2 + sub
            rs_copy(n - 2, chain).wait_recv()
            recon = sums[n - 1, chain].astype(jnp.float32) + own_term(way, sub) + bias_ref[:, wide]
            target_rows = pl.ds(chain * sub_rows, sub_rows)
            resid[pos, target_rows, :] = (
                2.0 / total_rows * (recon - acts[target_rows, :].astype(jnp.float32))
            ).astype(jnp.bfloat16)
            ag_copy(0, 0, chain).start()
            ag_copy(1, 0, chain).start()

    def compute(shard, sub, fresh=False):
        if sub >= pieces:
            return
        lat_slice = pl.ds(sub * piece, piece)
        block = resid[shard]
        term = lax.dot_general(
            block,
            dec_block(shard, lat_slice),
            (((1,), (1,)), ((), ())),
            preferred_element_type=jnp.float32,
        )
        if fresh:
            code_grad[:, lat_slice] = term
        else:
            code_grad[:, lat_slice] += term
        grad = jnp.dot(
            codes_t[lat_slice, :], block, preferred_element_type=jnp.float32
        ).astype(jnp.bfloat16)
        mine = shard // half == row

        @pl.when(mine)
        def _():
            own_ref[lat_slice, columns(shard)] = grad

        @pl.when(jnp.logical_not(mine))
        def _():
            outgoing[lax.rem(shard, half), lat_slice, :] = grad
            if sub == pieces - 1:
                exchange(lax.rem(shard, half)).start()

    def forward(step, sub):
        for way in range(2):
            ag_copy(way, step, sub).wait_recv()
            if sub // 2 == way:
                ag_copy(way, step + 1, sub).start()
            else:

                @pl.when(step < half - 2)
                def _():
                    ag_copy(way, step + 1, sub).start()

    for sub in range(subs):
        compute(pos, sub, fresh=True)
        forward(0, sub)

    @pl.loop(1, half - 1)
    def _(step):
        for sub in range(subs):
            compute(shard_at(-step), sub)
            compute(shard_at(step), sub)
            forward(step, sub)

    for sub in range(subs):
        compute(shard_at(1 - half), sub)
        compute(shard_at(half - 1), sub)
    for sub in range(subs):
        ag_copy(sub // 2, half - 1, sub).wait_recv()
    for sub in range(subs):
        compute(shard_at(half), sub)
    pre_grad_ref[...] = jnp.where(
        preact_ref[...] > 0, code_grad[...] + l1_weight / total_rows, 0.0
    ).astype(jnp.bfloat16)

    @pl.loop(0, n - 1)
    def _(step):
        for chain in range(subs):
            rs_copy(step, chain).wait_send()

    @pl.loop(0, half - 1)
    def _(step):
        for way in range(2):
            for sub in range(subs):
                ag_copy(way, step, sub).wait_send()

    for sub in range(subs):
        ag_copy(sub // 2, half - 1, sub).wait_send()

    @pl.loop(0, half)
    def _(block):
        exchange(block).wait_send()
        exchange(block).wait_recv()


def residual_step(preact, dec_own, dec_peer, dec_bias, activations, total_rows):
    n = lax.axis_size("lat")
    rows, lats = preact.shape
    model = activations.shape[1]
    width = model // n
    half = n // 2
    bf16, f32 = jnp.bfloat16, jnp.float32
    vmem = pl.BlockSpec(memory_space=pltpu.VMEM)
    whole = pl.BlockSpec(memory_space=pl.ANY)
    return pl.pallas_call(
        functools.partial(ring_kernel, n, n <= 8, total_rows),
        out_shape=(
            jax.ShapeDtypeStruct((rows, lats), bf16),
            jax.ShapeDtypeStruct((lats, model // 2), bf16),
            jax.ShapeDtypeStruct((lats, model // 2), bf16),
        ),
        in_specs=[vmem, whole, whole, vmem, whole],
        out_specs=(vmem, vmem, vmem),
        scratch_shapes=[
            pltpu.VMEM((2, lats, model // 2), bf16),
            pltpu.VMEM((rows, width), bf16),
            pltpu.VMEM((n, subs, rows // subs, width), bf16),
            pltpu.VMEM((n, rows, width), bf16),
            pltpu.VMEM((rows, lats), bf16),
            pltpu.VMEM((lats, rows), bf16),
            pltpu.VMEM((rows, lats), f32),
            pltpu.VMEM((2, rows // 2, width), f32),
            pltpu.VMEM((half, lats, width), bf16),
            pltpu.SemaphoreType.DMA((n - 1, subs)),
            pltpu.SemaphoreType.DMA((n - 1, subs)),
            pltpu.SemaphoreType.DMA((2, half, subs)),
            pltpu.SemaphoreType.DMA((2, half, subs)),
            pltpu.SemaphoreType.DMA((half,)),
            pltpu.SemaphoreType.DMA((half,)),
            pltpu.SemaphoreType.DMA((3,)),
        ],
        compiler_params=pltpu.CompilerParams(
            collective_id=0, has_side_effects=True, vmem_limit_bytes=58 * 1024 * 1024
        ),
        cost_estimate=pl.CostEstimate(
            flops=6 * rows * lats * model, bytes_accessed=30 * 1024 * 1024, transcendentals=0
        ),
    )(preact, dec_own, dec_peer, dec_bias.reshape(1, -1), activations)


def on_device(
    activations,
    enc_weight,
    dec_weight,
    enc_bias,
    dec_bias,
    enc_first,
    enc_second,
    dec_first,
    dec_second,
):
    total_rows = activations.shape[0] * lax.axis_size("row")
    row = lax.axis_index("row")
    part = enc_weight.shape[0]
    swap = [(0, 1), (1, 0)]
    enc_low = enc_weight.astype(jnp.bfloat16)
    enc_peer = lax.ppermute(enc_low, "row", swap)
    dec_low = dec_weight.astype(jnp.bfloat16)
    dec_peer = lax.ppermute(dec_low, "row", swap)

    centered = (activations.astype(jnp.float32) - dec_bias).astype(jnp.bfloat16)
    centered_own = lax.dynamic_slice_in_dim(centered, row * part, part, 1)
    centered_peer = lax.dynamic_slice_in_dim(centered, (1 - row) * part, part, 1)
    preact = jnp.dot(centered_own, enc_low, preferred_element_type=jnp.float32)
    preact = preact + jnp.dot(centered_peer, enc_peer, preferred_element_type=jnp.float32)
    preact = preact + enc_bias

    pre_grad, grad_dec_own, grad_dec_peer = residual_step(
        preact, dec_low, dec_peer, dec_bias, activations, total_rows
    )
    grad_out = rows_product(centered_peer, pre_grad).astype(jnp.bfloat16)
    grad_in = lax.ppermute(grad_out, "row", swap)
    dec_step = adam_step(
        grad_dec_own.astype(jnp.float32) + grad_dec_peer.astype(jnp.float32), dec_first, dec_second
    )
    grad_enc = rows_product(centered_own, pre_grad) + grad_in.astype(jnp.float32)
    return (adam_step(grad_enc, enc_first, enc_second), dec_step)


def solution(mesh):
    return jax.shard_map(
        on_device,
        mesh=mesh,
        in_specs=(
            P(("grp", "row"), None),
            P(("grp", "row"), "lat"),
            P(("grp", "lat"), "row"),
            P(("grp", "lat")),
            P("grp"),
            P(("grp", "row"), "lat"),
            P(("grp", "row"), "lat"),
            P(("grp", "lat"), "row"),
            P(("grp", "lat"), "row"),
        ),
        out_specs=(P(("grp", "row"), "lat"), P(("grp", "lat"), "row")),
        check_vma=False,
    )
```

time: 484 us -> 172 us (0.36)
  waiting for transfers between devices: 374 us -> 0.01 us
  Pallas kernels: 0 us -> 118 us
  matrix products: 63.3 us -> 30.3 us
  between operations: 13.8 us -> 0.73 us
  other arithmetic: 33.2 us -> 20.8 us
    psum x1 -> x0, waiting for transfers between devices: 329 us -> none  [on_device(): recon = lax.psum(partial_recon, 'lat') + dec_bias]
    pallas_call x0 -> x1, Pallas kernels: none -> 118 us  [residual_step(): pl.pallas_call(functools.partial(ring_kernel, n, n <= 8, total_rows), out...]
    all_gather x2 -> x0, waiting for transfers between devices: 30.1 us -> none  [the longest x1 16.5 us: on_device(): lax.all_gather(enc_low, 'row', axis=0, tiled=True)]
    dot_general x2, matrix products: 42.2 us -> 19.1 us  [rows_product(): lax.dot_general(left_rows, right_rows, (((0,), (0,)), ((), ())), preferre...]
    reduce_scatter x2 -> x0, waiting for transfers between devices: 14.6 us -> none  [the longest x1 14.6 us: on_device(): lax.psum_scatter(rows_product(col_block, pre_grad), 'row', scatter_dimens...]
    convert_element_type x2 -> x1, other arithmetic: 21 us -> 7.99 us  [adam_step(): return (scaled_one / (jnp.sqrt(scaled_two) + adam_eps)).astype(jnp.bfloat16)]
    dot_general x2, matrix products: 21 us -> 11.2 us  [the longest x1 6.57 us: on_device(): jnp.dot(centered_peer, enc_peer, preferred_element_type=jnp.float32)]
  transfers between devices with their start and end apart: 5 -> 3, of which waited for: 4 -> 0; matrix products, arithmetic and copies ran while one was open for 11% -> 15% of each run, Pallas kernels for 0% -> 0%
where the time goes in v1:
time: 172 us
  Pallas kernels  118 us (69%)
  matrix products  30.3 us (18%)
  other arithmetic  20.8 us (12%)
    pallas_call x1, Pallas kernels, residual_step(): pl.pallas_call(functools.partial(ring_kernel, n, n <= 8, total_rows), out...  118 us
    dot_general x2, matrix products, rows_product(): lax.dot_general(left_rows, right_rows, (((0,), (0,)), ((), ())), preferre...  19.1 us
    convert_element_type x1, other arithmetic, adam_step(): return (scaled_one / (jnp.sqrt(scaled_two) + adam_eps)).astype(jnp.bfloat16)  7.99 us
    dot_general x1, matrix products, on_device(): jnp.dot(centered_peer, enc_peer, preferred_element_type=jnp.float32)  6.57 us
    convert_element_type x1, other arithmetic, on_device(): enc_low = enc_weight.astype(jnp.bfloat16)  6.27 us
    dot_general x1, matrix products, on_device(): preact = jnp.dot(centered_own, enc_low, preferred_element_type=jnp.float32)  4.66 us
    convert_element_type x1, other arithmetic, on_device(): centered = (activations.astype(jnp.float32) - dec_bias).astype(jnp.bfloat16)  3.92 us
  transfers between devices with their start and end apart: 3, of which 0 were waited for; matrix products, arithmetic and copies ran while one was open for 15% of the time, Pallas kernels for 0%

profile of v1, /device:TPU:0, one launch (start us, length us, event | category | flops | bytes accessed | tf_op | source)
XLA Modules:
  0.0 172.2 jit_solution(11209728362309926868)
XLA Ops:
  0.6 0.0 copy-start
  0.6 6.3 %convert_element_type.45 = bf16[2048,1024]{1,0:T(8,128)(2,1)} convert(f32[2048,1024]{1,0:T(8,128)} %param.10) | non-fusion elementwise | flops 2097152 | bytes 12582912 | tf_op jit(solution)/shard_map/convert_element_type | solution.py:334
  6.9 0.0 copy-start.5
  6.9 0.5 collective-permute-start
  7.4 0.4 copy-done
  7.7 2.7 %convert_element_type.46.dec_own_ref = bf16[1024,2048]{1,0:T(8,128)(2,1)} convert(f32[1024,2048]{1,0:T(8,128)S(1)} %copy-done) | non-fusion elementwise | flops 2097152 | bytes 12582912 | tf_op jit(solution)/shard_map/convert_element_type | solution.py:336
  10.4 0.5 collective-permute-start.1
  10.8 0.0 copy-done.5
  10.8 3.9 %subtract_convert_fusion = bf16[640,4096]{1,0:T(8,128)(2,1)S(1)} fusion(bf16[640,4096]{1,0:T(8,128)(2,1)} %acts_ref.1, f32[4096]{0:T(1024)S(1)} %copy-done.5), kind=kLoop, calls=%fused_computation.2 | loop fusion | flops 7864320 | bytes 10502144 | tf_op jit(solution)/shard_map/convert_element_type | solution.py:339
  14.8 0.0 copy-start.8
  14.8 4.7 %fusion.16 = f32[640,1024]{1,0:T(8,128)S(1)} fusion(bf16[2048,1024]{1,0:T(8,128)(2,1)} %convert_element_type.45, bf16[640,4096]{1,0:T(8,128)(2,1)S(1)} %subtract_convert_fusion, s32[]{:T(128)S(6)} %select_n.6), kind=kOutput, calls=%fused_computation.21 | convolution fusion | flops 2684354560 | bytes 9437188 | tf_op jit(solution)/shard_map/dot_general | solution.py:342
  19.5 0.0 collective-permute-done
  19.5 0.0 copy-done.8
  19.5 6.6 %add_add_fusion.preact_ref = f32[640,1024]{1,0:T(8,128)} fusion(f32[640,1024]{1,0:T(8,128)S(1)} %fusion.16, bf16[2048,1024]{1,0:T(8,128)(2,1)} %collective-permute-done, bf16[640,4096]{1,0:T(8,128)(2,1)S(1)} %subtract_convert_fusion, s32[]{:T(128)S(6)} %select_n.7, f32[1024]{0:T(1024)S(1)} %copy-done.8), kind=kOutput, calls=%fused_computation.16 | convolution fusion | flops 2685665280 | bytes 12062724 | tf_op jit(solution)/shard_map/dot_general | solution.py:343
  26.0 0.0 collective-permute-done.1.dec_peer_ref
  26.1 117.8 %shard_map.104 = (bf16[640,1024]{1,0:T(8,128)(2,1)}, bf16[1024,2048]{1,0:T(8,128)(2,1)}, bf16[1024,2048]{1,0:T(8,128)(2,1)}) custom-call(f32[640,1024]{1,0:T(8,128)} %add_add_fusion.preact_ref, bf16[1024,2048]{1,0:T(8,128)(2,1)} %convert_element_type.46.dec_own_ref, bf16[1024,2048]{1,0:T(8,128)(2,1)} %collective-permute-done.1.dec_peer_ref, ...), custom_call_target="tpu_custom_call" | custom-call | flops 16106127360 | bytes 31457280 | tf_op jit(solution)/shard_map/pallas_call | solution.py:283
  143.9 0.0 copy-start.1
  143.9 0.0 copy-start.2
  143.9 0.0 copy-start.3
  143.9 0.0 copy-start.4
  143.9 6.5 %convolution_convert_fusion = bf16[2048,1024]{1,0:T(8,128)(2,1)} fusion(bf16[640,1024]{1,0:T(8,128)(2,1)} %get-tuple-element.5, bf16[640,4096]{1,0:T(8,128)(2,1)S(1)} %subtract_convert_fusion, s32[]{:T(128)S(6)} %select_n.7), kind=kOutput, calls=%fused_computation.15 | convolution fusion | flops 2686451712 | bytes 8126468 | tf_op jit(solution)/shard_map/dot_general | solution.py:27
  150.4 0.4 collective-permute-start.2
  150.8 0.0 copy-done.1
  150.8 0.0 copy-done.2
  150.8 0.0 copy-done.3
  150.8 0.8 copy-done.4
  151.7 0.0 copy-start.6
  151.7 0.0 copy-start.7
  151.7 8.0 %fusion.10 = bf16[1024,2048]{1,0:T(8,128)(2,1)} fusion(bf16[1024,2048]{1,0:T(8,128)(2,1)S(1)} %copy-done.1, bf16[1024,2048]{1,0:T(8,128)(2,1)S(1)} %copy-done.4, bf16[1024,2048]{1,0:T(8,128)(2,1)S(1)} %copy-done.3, bf16[1024,2048]{1,0:T(8,128)(2,1)S(1)} %copy-done.2), kind=kLoop, calls=%fused_computation.13 | loop fusion | flops 33554432 | bytes 20971520 | tf_op jit(solution)/shard_map/convert_element_type | solution.py:23
  159.7 0.0 collective-permute-done.2
  159.7 0.0 copy-done.6
  159.7 0.0 copy-done.7
  159.7 12.6 %fusion.11 = bf16[2048,1024]{1,0:T(8,128)(2,1)} fusion(bf16[2048,1024]{1,0:T(8,128)(2,1)S(1)} %copy-done.6, bf16[2048,1024]{1,0:T(8,128)(2,1)} %collective-permute-done.2, bf16[2048,1024]{1,0:T(8,128)(2,1)S(1)} %copy-done.7, bf16[640,1024]{1,0:T(8,128)(2,1)} %get-tuple-element.5, bf16[640,4096]{1,0:T(8,128)(2,1)S(1)} %subtract_convert_fusion, s32[]{:T(128)S(6)} %select_n.6), kind=kOutput, calls=%fused_computation.14 | convolution fusion | flops 2715811840 | bytes 20709380 | tf_op jit(solution)/shard_map/dot_general | solution.py:27
Async XLA Ops:
  0.6 7.1 %copy-start = (f32[1024,2048]{1,0:T(8,128)S(1)}, f32[1024,2048]{1,0:T(8,128)}, u32[]{:S(2)}) copy-start(f32[1024,2048]{1,0:T(8,128)} %param.11) | copy-start | bytes 25165828
  6.9 3.9 %copy-start.5 = (f32[4096]{0:T(1024)S(1)}, f32[4096]{0:T(1024)}, u32[]{:S(2)}) copy-start(f32[4096]{0:T(1024)} %param.13) | copy-start | bytes 49156
  6.9 12.6 %collective-permute-start = (bf16[2048,1024]{1,0:T(8,128)(2,1)}, bf16[2048,1024]{1,0:T(8,128)(2,1)}, u32[]{:S(2)}, u32[]{:S(2)}) collective-permute-start(bf16[2048,1024]{1,0:T(8,128)(2,1)} %convert_element_type.45), channel_id=1, source_target_pairs={{0,1},{1,0},{2,3},{3,2},{4,5},{5,4},{6,7},{7,6},{8,9},{9,8},{10,11... | collective-permute-start | bytes 12582920 | tf_op jit(solution)/shard_map/ppermute | solution.py:335
  10.4 15.7 %collective-permute-start.1 = (bf16[1024,2048]{1,0:T(8,128)(2,1)}, bf16[1024,2048]{1,0:T(8,128)(2,1)}, u32[]{:S(2)}, u32[]{:S(2)}) collective-permute-start(bf16[1024,2048]{1,0:T(8,128)(2,1)} %convert_element_type.46.dec_own_ref), channel_id=1, source_target_pairs={{0,1},{1,0},{2,3},{3,2},{4,5},{5,4},{6,7},{7,6},{8,9},{9,8},{10,11... | collective-permute-start | bytes 12582920 | tf_op jit(solution)/shard_map/ppermute | solution.py:337
  14.8 4.7 %copy-start.8 = (f32[1024]{0:T(1024)S(1)}, f32[1024]{0:T(1024)}, u32[]{:S(2)}) copy-start(f32[1024]{0:T(1024)} %param.12) | copy-start | bytes 12292
  143.9 6.9 %copy-start.1 = (bf16[1024,2048]{1,0:T(8,128)(2,1)S(1)}, bf16[1024,2048]{1,0:T(8,128)(2,1)}, u32[]{:S(2)}) copy-start(bf16[1024,2048]{1,0:T(8,128)(2,1)} %param.17) | copy-start | bytes 12582916
  143.9 6.9 %copy-start.2 = (bf16[1024,2048]{1,0:T(8,128)(2,1)S(1)}, bf16[1024,2048]{1,0:T(8,128)(2,1)}, u32[]{:S(2)}) copy-start(bf16[1024,2048]{1,0:T(8,128)(2,1)} %param.16) | copy-start | bytes 12582916
  143.9 6.9 %copy-start.3 = (bf16[1024,2048]{1,0:T(8,128)(2,1)S(1)}, bf16[1024,2048]{1,0:T(8,128)(2,1)}, u32[]{:S(2)}) copy-start(bf16[1024,2048]{1,0:T(8,128)(2,1)} %get-tuple-element.6) | copy-start | bytes 12582916
  143.9 7.7 %copy-start.4 = (bf16[1024,2048]{1,0:T(8,128)(2,1)S(1)}, bf16[1024,2048]{1,0:T(8,128)(2,1)}, u32[]{:S(2)}) copy-start(bf16[1024,2048]{1,0:T(8,128)(2,1)} %get-tuple-element.7) | copy-start | bytes 12582916
  150.4 9.2 %collective-permute-start.2 = (bf16[2048,1024]{1,0:T(8,128)(2,1)}, bf16[2048,1024]{1,0:T(8,128)(2,1)}, u32[]{:S(2)}, u32[]{:S(2)}) collective-permute-start(bf16[2048,1024]{1,0:T(8,128)(2,1)} %convolution_convert_fusion), channel_id=1, source_target_pairs={{0,1},{1,0},{2,3},{3,2},{4,5},{5,4},{6,7},{7,6},{8,9},{9,8},{10,11... | collective-permute-start | bytes 12582920 | tf_op jit(solution)/shard_map/ppermute | solution.py:350
  151.7 8.0 %copy-start.6 = (bf16[2048,1024]{1,0:T(8,128)(2,1)S(1)}, bf16[2048,1024]{1,0:T(8,128)(2,1)}, u32[]{:S(2)}) copy-start(bf16[2048,1024]{1,0:T(8,128)(2,1)} %param.15) | copy-start | bytes 12582916
  151.7 8.0 %copy-start.7 = (bf16[2048,1024]{1,0:T(8,128)(2,1)S(1)}, bf16[2048,1024]{1,0:T(8,128)(2,1)}, u32[]{:S(2)}) copy-start(bf16[2048,1024]{1,0:T(8,128)(2,1)} %param.14) | copy-start | bytes 12582916

commit v2 on v1

--- a/solution.py
+++ b/solution.py
@@ -13,6 +13,7 @@
 adam_eps = 1e-08
 step_count = 1000.0
 subs = 4
+blocks = 8
 
 
 def adam_step(gradient, first, second):
@@ -33,14 +34,20 @@
     n,
     snake,
     total_rows,
-    preact_ref,
-    dec_own_ref,
-    dec_peer_ref,
+    enc_ref,
+    dec_ref,
+    enc_bias_ref,
     bias_ref,
     acts_ref,
     pre_grad_ref,
     own_ref,
     recv_ref,
+    centered_ref,
+    preact,
+    centered,
+    enc,
+    enc_stage,
+    dec_stage,
     dec,
     acts,
     sums,
@@ -57,8 +64,15 @@
     x_send,
     x_recv,
     load_sem,
+    enc_load,
+    dec_load,
+    enc_send,
+    enc_recv,
+    dec_send,
+    dec_recv,
+    keep_sem,
 ):
-    rows, lats = preact_ref.shape
+    rows, lats = preact.shape
     width = resid.shape[2]
     half = n // 2
     sub_rows = rows // subs
@@ -94,17 +108,105 @@
     def columns(shard):
         return pl.ds(pl.multiple_of(lax.rem(shard, half) * width, width), width)
 
-    load_own = pltpu.make_async_copy(dec_own_ref, dec.at[row], load_sem.at[0])
-    load_peer = pltpu.make_async_copy(dec_peer_ref, dec.at[1 - row], load_sem.at[1])
     wide = pl.ds(pl.multiple_of(pos * width, width), width)
-    load_acts = pltpu.make_async_copy(acts_ref.at[:, wide], acts, load_sem.at[2])
-    load_own.start()
-    load_peer.start()
+    load_acts = pltpu.make_async_copy(acts_ref.at[:, wide], acts, load_sem.at[0])
+    load_all = pltpu.make_async_copy(acts_ref, centered, load_sem.at[1])
+    save_centered = pltpu.make_async_copy(centered, centered_ref, load_sem.at[2])
+    enc_rows = enc_stage.shape[1]
+    dec_rows = dec_stage.shape[1]
+    model_half = enc_ref.shape[0]
+
+    def load_enc(block):
+        return pltpu.make_async_copy(
+            enc_ref.at[pl.ds(block * enc_rows, enc_rows), :],
+            enc_stage.at[lax.rem(block, 2)],
+            enc_load.at[lax.rem(block, 2)],
+        )
+
+    def load_dec(block):
+        return pltpu.make_async_copy(
+            dec_ref.at[pl.ds(block * dec_rows, dec_rows), :],
+            dec_stage.at[lax.rem(block, 2)],
+            dec_load.at[lax.rem(block, 2)],
+        )
+
+    def swap_enc(block):
+        place = enc.at[row, pl.ds(block * enc_rows, enc_rows), :]
+        return pltpu.make_async_remote_copy(
+            src_ref=place,
+            dst_ref=place,
+            send_sem=enc_send.at[block],
+            recv_sem=enc_recv.at[block],
+            device_id={"row": 1 - row},
+            device_id_type=pl.DeviceIdType.MESH,
+        )
+
+    def swap_dec(block):
+        place = dec.at[row, pl.ds(block * dec_rows, dec_rows), :]
+        return pltpu.make_async_remote_copy(
+            src_ref=place,
+            dst_ref=place,
+            send_sem=dec_send.at[block],
+            recv_sem=dec_recv.at[block],
+            device_id={"row": 1 - row},
+            device_id_type=pl.DeviceIdType.MESH,
+        )
+
+    load_all.start()
+    load_enc(0).start()
+    load_enc(1).start()
+    load_dec(0).start()
+    load_dec(1).start()
     load_acts.start()
-    codes[...] = jnp.maximum(preact_ref[...], 0.0).astype(jnp.bfloat16)
-    load_own.wait()
-    load_peer.wait()
+    preact[...] = jnp.broadcast_to(enc_bias_ref[...], preact.shape)
     pl.semaphore_wait(barrier, 3)
+    load_all.wait()
+
+    def encode(owner, block):
+        place = pl.ds(pl.multiple_of(owner * model_half + block * enc_rows, enc_rows), enc_rows)
+        chunk = (centered[:, place].astype(jnp.float32) - bias_ref[:, place]).astype(jnp.bfloat16)
+        centered[:, place] = chunk
+        preact[...] += jnp.dot(
+            chunk,
+            enc[owner, pl.ds(block * enc_rows, enc_rows), :],
+            preferred_element_type=jnp.float32,
+        )
+
+    @pl.loop(0, blocks)
+    def _(block):
+        load_enc(block).wait()
+        enc[row, pl.ds(block * enc_rows, enc_rows), :] = enc_stage[lax.rem(block, 2)].astype(
+            jnp.bfloat16
+        )
+        swap_enc(block).start()
+
+        @pl.when(block < blocks - 2)
+        def _():
+            load_enc(block + 2).start()
+
+        load_dec(block).wait()
+        dec[row, pl.ds(block * dec_rows, dec_rows), :] = dec_stage[lax.rem(block, 2)].astype(
+            jnp.bfloat16
+        )
+        swap_dec(block).start()
+
+        @pl.when(block < blocks - 2)
+        def _():
+            load_dec(block + 2).start()
+
+        encode(row, block)
+
+    @pl.loop(0, blocks)
+    def _(block):
+        swap_enc(block).wait_recv()
+        encode(1 - row, block)
+
+    save_centered.start()
+    codes[...] = jnp.maximum(preact[...], 0.0).astype(jnp.bfloat16)
+
+    @pl.loop(0, blocks)
+    def _(block):
+        swap_dec(block).wait_recv()
 
     def dec_block(shard, lat_slice=slice(None)):
         return dec[shard // half, lat_slice, columns(shard)]
@@ -141,12 +243,18 @@
     def exchange(block):
         place = pl.ds(pl.multiple_of(block * width, width), width)
         return pltpu.make_async_remote_copy(
-            src_ref=outgoing.at[block],
+            src_ref=outgoing.at[(1 - row) * half + block],
             dst_ref=recv_ref.at[:, place],
             send_sem=x_send.at[block],
             recv_sem=x_recv.at[block],
             device_id={"row": 1 - row},
             device_id_type=pl.DeviceIdType.MESH,
+        )
+
+    def keep(block):
+        place = pl.ds(pl.multiple_of(block * width, width), width)
+        return pltpu.make_async_copy(
+            outgoing.at[row * half + block], own_ref.at[:, place], keep_sem.at[block]
         )
 
     for way in range(2):
@@ -155,7 +263,7 @@
             chain = way * 2 + sub
             sums[0, chain] = first[sub * sub_rows : (sub + 1) * sub_rows].astype(jnp.bfloat16)
             rs_copy(0, chain).start()
-    codes_t[...] = jnp.maximum(jnp.transpose(preact_ref[...]), 0.0).astype(jnp.bfloat16)
+    codes_t[...] = jnp.maximum(jnp.transpose(preact[...]), 0.0).astype(jnp.bfloat16)
 
     def own_term(way, sub):
         return part[way, pl.ds(sub * sub_rows, sub_rows), :]
@@ -206,16 +314,16 @@
         grad = jnp.dot(
             codes_t[lat_slice, :], block, preferred_element_type=jnp.float32
         ).astype(jnp.bfloat16)
-        mine = shard // half == row
-
-        @pl.when(mine)
-        def _():
-            own_ref[lat_slice, columns(shard)] = grad
-
-        @pl.when(jnp.logical_not(mine))
-        def _():
-            outgoing[lax.rem(shard, half), lat_slice, :] = grad
-            if sub == pieces - 1:
+        outgoing[shard, lat_slice, :] = grad
+        if sub == pieces - 1:
+            mine = shard // half == row
+
+            @pl.when(mine)
+            def _():
+                keep(lax.rem(shard, half)).start()
+
+            @pl.when(jnp.logical_not(mine))
+            def _():
                 exchange(lax.rem(shard, half)).start()
 
     def forward(step, sub):
@@ -248,7 +356,7 @@
     for sub in range(subs):
         compute(shard_at(half), sub)
     pre_grad_ref[...] = jnp.where(
-        preact_ref[...] > 0, code_grad[...] + l1_weight / total_rows, 0.0
+        preact[...] > 0, code_grad[...] + l1_weight / total_rows, 0.0
     ).astype(jnp.bfloat16)
 
     @pl.loop(0, n - 1)
@@ -269,12 +377,20 @@
     def _(block):
         exchange(block).wait_send()
         exchange(block).wait_recv()
-
-
-def residual_step(preact, dec_own, dec_peer, dec_bias, activations, total_rows):
+        keep(block).wait()
+
+    @pl.loop(0, blocks)
+    def _(block):
+        swap_enc(block).wait_send()
+        swap_dec(block).wait_send()
+
+    save_centered.wait()
+
+
+def residual_step(enc_weight, dec_weight, enc_bias, dec_bias, activations, total_rows):
     n = lax.axis_size("lat")
-    rows, lats = preact.shape
-    model = activations.shape[1]
+    rows, model = activations.shape
+    lats = enc_weight.shape[1]
     width = model // n
     half = n // 2
     bf16, f32 = jnp.bfloat16, jnp.float32
@@ -286,10 +402,16 @@
             jax.ShapeDtypeStruct((rows, lats), bf16),
             jax.ShapeDtypeStruct((lats, model // 2), bf16),
             jax.ShapeDtypeStruct((lats, model // 2), bf16),
+            jax.ShapeDtypeStruct((rows, model), bf16),
         ),
-        in_specs=[vmem, whole, whole, vmem, whole],
-        out_specs=(vmem, vmem, vmem),
+        in_specs=[whole, whole, vmem, vmem, whole],
+        out_specs=(vmem, whole, whole, whole),
         scratch_shapes=[
+            pltpu.VMEM((rows, lats), f32),
+            pltpu.VMEM((rows, model), bf16),
+            pltpu.VMEM((2, model // 2, lats), bf16),
+            pltpu.VMEM((2, model // 2 // blocks, lats), f32),
+            pltpu.VMEM((2, lats // blocks, model // 2), f32),
             pltpu.VMEM((2, lats, model // 2), bf16),
             pltpu.VMEM((rows, width), bf16),
             pltpu.VMEM((n, subs, rows // subs, width), bf16),
@@ -298,7 +420,7 @@
             pltpu.VMEM((lats, rows), bf16),
             pltpu.VMEM((rows, lats), f32),
             pltpu.VMEM((2, rows // 2, width), f32),
-            pltpu.VMEM((half, lats, width), bf16),
+            pltpu.VMEM((n, lats, width), bf16),
             pltpu.SemaphoreType.DMA((n - 1, subs)),
             pltpu.SemaphoreType.DMA((n - 1, subs)),
             pltpu.SemaphoreType.DMA((2, half, subs)),
@@ -306,14 +428,21 @@
             pltpu.SemaphoreType.DMA((half,)),
             pltpu.SemaphoreType.DMA((half,)),
             pltpu.SemaphoreType.DMA((3,)),
+            pltpu.SemaphoreType.DMA((2,)),
+            pltpu.SemaphoreType.DMA((2,)),
+            pltpu.SemaphoreType.DMA((blocks,)),
+            pltpu.SemaphoreType.DMA((blocks,)),
+            pltpu.SemaphoreType.DMA((blocks,)),
+            pltpu.SemaphoreType.DMA((blocks,)),
+            pltpu.SemaphoreType.DMA((half,)),
         ],
         compiler_params=pltpu.CompilerParams(
-            collective_id=0, has_side_effects=True, vmem_limit_bytes=58 * 1024 * 1024
+            collective_id=0, has_side_effects=True, vmem_limit_bytes=60 * 1024 * 1024
         ),
         cost_estimate=pl.CostEstimate(
-            flops=6 * rows * lats * model, bytes_accessed=30 * 1024 * 1024, transcendentals=0
+            flops=8 * rows * lats * model, bytes_accessed=30 * 1024 * 1024, transcendentals=0
         ),
-    )(preact, dec_own, dec_peer, dec_bias.reshape(1, -1), activations)
+    )(enc_weight, dec_weight, enc_bias.reshape(1, -1), dec_bias.reshape(1, -1), activations)
 
 
 def on_device(
@@ -331,21 +460,11 @@
     row = lax.axis_index("row")
     part = enc_weight.shape[0]
     swap = [(0, 1), (1, 0)]
-    enc_low = enc_weight.astype(jnp.bfloat16)
-    enc_peer = lax.ppermute(enc_low, "row", swap)
-    dec_low = dec_weight.astype(jnp.bfloat16)
-    dec_peer = lax.ppermute(dec_low, "row", swap)
-
-    centered = (activations.astype(jnp.float32) - dec_bias).astype(jnp.bfloat16)
+    pre_grad, grad_dec_own, grad_dec_peer, centered = residual_step(
+        enc_weight, dec_weight, enc_bias, dec_bias, activations, total_rows
+    )
     centered_own = lax.dynamic_slice_in_dim(centered, row * part, part, 1)
     centered_peer = lax.dynamic_slice_in_dim(centered, (1 - row) * part, part, 1)
-    preact = jnp.dot(centered_own, enc_low, preferred_element_type=jnp.float32)
-    preact = preact + jnp.dot(centered_peer, enc_peer, preferred_element_type=jnp.float32)
-    preact = preact + enc_bias
-
-    pre_grad, grad_dec_own, grad_dec_peer = residual_step(
-        preact, dec_low, dec_peer, dec_bias, activations, total_rows
-    )
     grad_out = rows_product(centered_peer, pre_grad).astype(jnp.bfloat16)
     grad_in = lax.ppermute(grad_out, "row", swap)
     dec_step = adam_step(

time: 172 us -> 160 us (0.930)
  matrix products: 30.3 us -> 20.1 us
  other arithmetic: 20.8 us -> 11.6 us
  Pallas kernels: 118 us -> 127 us
    convert_element_type x3 -> x0, other arithmetic: 12.8 us -> none  [the longest x1 6.27 us: on_device(): enc_low = enc_weight.astype(jnp.bfloat16)]
    dot_general x2 -> x0, matrix products: 11.2 us -> none  [the longest x1 6.57 us: on_device(): jnp.dot(centered_peer, enc_peer, preferred_element_type=jnp.float32)]
    pallas_call x1, Pallas kernels: 118 us -> 127 us  [residual_step(): pl.pallas_call(functools.partial(ring_kernel, n, n <= 8, total_rows), out...]
    convert_element_type x1, other arithmetic: 7.99 us -> 11.6 us  [adam_step(): return (scaled_one / (jnp.sqrt(scaled_two) + adam_eps)).astype(jnp.bfloat16)]
  transfers between devices with their start and end apart: 3 -> 1, of which waited for: 0 -> 0; matrix products, arithmetic and copies ran while one was open for 15% -> 7% of each run, Pallas kernels for 0% -> 0%
where the time goes in v2:
time: 160 us
  Pallas kernels  127 us (79%)
  matrix products  20.1 us (13%)
  other arithmetic  11.6 us (7%)
    pallas_call x1, Pallas kernels, residual_step(): pl.pallas_call(functools.partial(ring_kernel, n, n <= 8, total_rows), out...  127 us
    dot_general x2, matrix products, rows_product(): lax.dot_general(left_rows, right_rows, (((0,), (0,)), ((), ())), preferre...  20.1 us
    convert_element_type x1, other arithmetic, adam_step(): return (scaled_one / (jnp.sqrt(scaled_two) + adam_eps)).astype(jnp.bfloat16)  11.6 us
  transfers between devices with their start and end apart: 1, of which 0 were waited for; matrix products, arithmetic and copies ran while one was open for 7% of the time, Pallas kernels for 0%

profile of v2, /device:TPU:0, one launch (start us, length us, event | category | flops | bytes accessed | tf_op | source)
XLA Modules:
  0.0 159.5 jit_solution(1976014061824340062)
XLA Ops:
  0.6 126.8 %shard_map.104 = (bf16[640,1024]{1,0:T(8,128)(2,1)}, bf16[1024,2048]{1,0:T(8,128)(2,1)}, bf16[1024,2048]{1,0:T(8,128)(2,1)}, bf16[640,4096]{1,0:T(8,128)(2,1)}) custom-call(f32[2048,1024]{1,0:T(8,128)} %enc_ref.1, f32[1024,2048]{1,0:T(8,128)} %dec_ref.1, f32[1,1024]{1,0:T(1,128)} %bitcast.5, f32[1,4096]{1,0:T(1,128)} %bitcast.4, bf16[640,4096]{1,0:T(8,128)(2,1)} %acts_ref.1), custom_call_target="tpu_custom_call" | custom-call | flops 21474836480 | bytes 31457280 | tf_op jit(solution)/shard_map/pallas_call | solution.py:399
  127.4 0.0 slice-start
  127.4 7.7 %convolution_convert_fusion = bf16[2048,1024]{1,0:T(8,128)(2,1)} fusion(bf16[640,1024]{1,0:T(8,128)(2,1)} %get-tuple-element.7, bf16[640,4096]{1,0:T(8,128)(2,1)} %get-tuple-element.6, s32[]{:T(128)S(6)} %select_n.7), kind=kOutput, calls=%fused_computation.14 | convolution fusion | flops 2686451712 | bytes 8126468 | tf_op jit(solution)/shard_map/dot_general | solution.py:28
  135.1 0.4 collective-permute-start
  135.5 0.0 copy-start
  135.5 0.0 copy-start.1
  135.5 0.0 slice-start.1
  135.5 0.0 copy-start.2
  135.5 11.6 %fusion.10 = bf16[1024,2048]{1,0:T(8,128)(2,1)} fusion(bf16[1024,2048]{1,0:T(8,128)(2,1)} %param.17, bf16[1024,2048]{1,0:T(8,128)(2,1)} %get-tuple-element.9, bf16[1024,2048]{1,0:T(8,128)(2,1)} %get-tuple-element.8, bf16[1024,2048]{1,0:T(8,128)(2,1)} %param.16), kind=kLoop, calls=%fused_computation.12 | loop fusion | flops 33554432 | bytes 20971520 | tf_op jit(solution)/shard_map/convert_element_type | solution.py:24
  147.0 0.0 collective-permute-done
  147.0 0.0 slice-done
  147.0 0.0 copy-done
  147.1 0.0 copy-done.1
  147.1 0.0 slice-done.1
  147.1 0.0 copy-done.2
  147.1 12.4 %fusion.11 = bf16[2048,1024]{1,0:T(8,128)(2,1)} fusion(bf16[2048,1024]{1,0:T(8,128)(2,1)S(1)} %copy-done, bf16[2048,1024]{1,0:T(8,128)(2,1)} %collective-permute-done, bf16[2048,1024]{1,0:T(8,128)(2,1)S(1)} %copy-done.1, bf16[640,1024]{1,0:T(8,128)(2,1)S(1)} %copy-done.2, bf16[640,4096]{1,0:T(8,128)(2,1)S(1)} %bitcast.7, s32[]{:T(128)S(6)} %select_n.6), kind=kOutput, calls=%fused_computation.13 | convolution fusion | flops 2715811840 | bytes 20709380 | tf_op jit(solution)/shard_map/dot_general | solution.py:28
  (1 shorter events, 0.0 us)
Async XLA Ops:
  127.4 19.6 %slice-start = ((s8[5242880]{0:T(1024)(128)(4,1)}), s8[1048576]{0:T(1024)(128)(4,1)S(1)}, s32[]{:S(2)}) async-start(s8[5242880]{0:T(1024)(128)(4,1)} %bitcast.6), calls=%async_computation | async-start | bytes 2097152
  135.1 11.9 %collective-permute-start = (bf16[2048,1024]{1,0:T(8,128)(2,1)}, bf16[2048,1024]{1,0:T(8,128)(2,1)}, u32[]{:S(2)}, u32[]{:S(2)}) collective-permute-start(bf16[2048,1024]{1,0:T(8,128)(2,1)} %convolution_convert_fusion), channel_id=1, source_target_pairs={{0,1},{1,0},{2,3},{3,2},{4,5},{5,4},{6,7},{7,6},{8,9},{9,8},{10,11... | collective-permute-start | bytes 12582920 | tf_op jit(solution)/shard_map/ppermute | solution.py:469
  135.5 11.6 %copy-start = (bf16[2048,1024]{1,0:T(8,128)(2,1)S(1)}, bf16[2048,1024]{1,0:T(8,128)(2,1)}, u32[]{:S(2)}) copy-start(bf16[2048,1024]{1,0:T(8,128)(2,1)} %param.15) | copy-start | bytes 12582916
  135.5 11.6 %copy-start.1 = (bf16[2048,1024]{1,0:T(8,128)(2,1)S(1)}, bf16[2048,1024]{1,0:T(8,128)(2,1)}, u32[]{:S(2)}) copy-start(bf16[2048,1024]{1,0:T(8,128)(2,1)} %param.14) | copy-start | bytes 12582916
  135.5 11.6 %slice-start.1 = ((s8[5242880]{0:T(1024)(128)(4,1)}), s8[4194304]{0:T(1024)(128)(4,1)S(1)}, s32[]{:S(2)}) async-start(s8[5242880]{0:T(1024)(128)(4,1)} %bitcast.6), calls=%async_computation.1 | async-start | bytes 8388608
  135.5 11.6 %copy-start.2 = (bf16[640,1024]{1,0:T(8,128)(2,1)S(1)}, bf16[640,1024]{1,0:T(8,128)(2,1)}, u32[]{:S(2)}) copy-start(bf16[640,1024]{1,0:T(8,128)(2,1)} %get-tuple-element.7) | copy-start | bytes 3932164

commit v3 on v2

--- a/solution.py
+++ b/solution.py
@@ -14,6 +14,7 @@
 step_count = 1000.0
 subs = 4
 blocks = 8
+chunk_rows = 32
 
 
 def adam_step(gradient, first, second):
@@ -39,9 +40,10 @@
     enc_bias_ref,
     bias_ref,
     acts_ref,
+    first_ref,
+    second_ref,
     pre_grad_ref,
-    own_ref,
-    recv_ref,
+    step_ref,
     centered_ref,
     preact,
     centered,
@@ -71,6 +73,8 @@
     dec_send,
     dec_recv,
     keep_sem,
+    moment_sem,
+    arrived,
 ):
     rows, lats = preact.shape
     width = resid.shape[2]
@@ -106,9 +110,11 @@
         return lax.rem(pos + offset + 2 * n, n)
 
     def columns(shard):
-        return pl.ds(pl.multiple_of(lax.rem(shard, half) * width, width), width)
-
-    wide = pl.ds(pl.multiple_of(pos * width, width), width)
+        return pl.ds(pl.multiple_of(shard // 2 * width, width), width)
+
+    wide = pl.ds(
+        pl.multiple_of(lax.rem(pos, 2) * enc_ref.shape[0] + pos // 2 * width, width), width
+    )
     load_acts = pltpu.make_async_copy(acts_ref.at[:, wide], acts, load_sem.at[0])
     load_all = pltpu.make_async_copy(acts_ref, centered, load_sem.at[1])
     save_centered = pltpu.make_async_copy(centered, centered_ref, load_sem.at[2])
@@ -184,15 +190,17 @@
         def _():
             load_enc(block + 2).start()
 
-        load_dec(block).wait()
-        dec[row, pl.ds(block * dec_rows, dec_rows), :] = dec_stage[lax.rem(block, 2)].astype(
-            jnp.bfloat16
-        )
-        swap_dec(block).start()
-
-        @pl.when(block < blocks - 2)
-        def _():
-            load_dec(block + 2).start()
+        for piece_of in range(2):
+            lower = 2 * block + piece_of
+            load_dec(lower).wait()
+            dec[row, pl.ds(lower * dec_rows, dec_rows), :] = dec_stage[piece_of].astype(
+                jnp.bfloat16
+            )
+            swap_dec(lower).start()
+
+            @pl.when(block < blocks - 1)
+            def _():
+                load_dec(lower + 2).start()
 
         encode(row, block)
 
@@ -204,12 +212,12 @@
     save_centered.start()
     codes[...] = jnp.maximum(preact[...], 0.0).astype(jnp.bfloat16)
 
-    @pl.loop(0, blocks)
+    @pl.loop(0, 2 * blocks)
     def _(block):
         swap_dec(block).wait_recv()
 
     def dec_block(shard, lat_slice=slice(None)):
-        return dec[shard // half, lat_slice, columns(shard)]
+        return dec[lax.rem(shard, 2), lat_slice, columns(shard)]
 
     def partial(way, shard):
         return jnp.dot(
@@ -241,10 +249,9 @@
         )
 
     def exchange(block):
-        place = pl.ds(pl.multiple_of(block * width, width), width)
         return pltpu.make_async_remote_copy(
-            src_ref=outgoing.at[(1 - row) * half + block],
-            dst_ref=recv_ref.at[:, place],
+            src_ref=outgoing.at[2 * block + 1 - row],
+            dst_ref=arrived.at[block],
             send_sem=x_send.at[block],
             recv_sem=x_recv.at[block],
             device_id={"row": 1 - row},
@@ -254,8 +261,55 @@
     def keep(block):
         place = pl.ds(pl.multiple_of(block * width, width), width)
         return pltpu.make_async_copy(
-            outgoing.at[row * half + block], own_ref.at[:, place], keep_sem.at[block]
-        )
+            outgoing.at[2 * block + row], step_ref.at[:, place], keep_sem.at[block]
+        )
+
+    across = lats // width
+
+    def moment_place(block, start, size):
+        return (
+            pl.ds(pl.multiple_of(block // across * lats + start, chunk_rows), size),
+            pl.ds(pl.multiple_of(lax.rem(block, across) * width, width), width),
+        )
+
+    def load_moment(which, block):
+        source = (first_ref, second_ref)[which]
+        place = pl.ds(pl.multiple_of(block * width, width), width)
+        down, along = moment_place(block, 0, lats)
+        return pltpu.make_async_copy(
+            source.at[:, place], enc.at[which, down, along], moment_sem.at[which, block]
+        )
+
+    @pl.loop(0, blocks)
+    def _(block):
+        swap_enc(block).wait_send()
+
+    @pl.loop(0, half)
+    def _(block):
+        load_moment(0, block).start()
+        load_moment(1, block).start()
+
+    def adam_block(shard):
+        block = shard // 2
+
+        @pl.when(lax.rem(shard, 2) == row)
+        def _():
+            load_moment(0, block).wait()
+            load_moment(1, block).wait()
+            exchange(block).wait_recv()
+
+            @pl.loop(0, lats // chunk_rows)
+            def _(chunk):
+                start = pl.multiple_of(chunk * chunk_rows, chunk_rows)
+                lines = pl.ds(start, chunk_rows)
+                down, along = moment_place(block, start, chunk_rows)
+                grad = outgoing[shard, lines, :].astype(jnp.float32)
+                grad = grad + arrived[block, lines, :].astype(jnp.float32)
+                outgoing[shard, lines, :] = adam_step(
+                    grad, enc[0, down, along], enc[1, down, along]
+                )
+
+            keep(block).start()
 
     for way in range(2):
         first = partial(way, shard_at(-1 if way == 0 else 1))
@@ -316,15 +370,9 @@
         ).astype(jnp.bfloat16)
         outgoing[shard, lat_slice, :] = grad
         if sub == pieces - 1:
-            mine = shard // half == row
-
-            @pl.when(mine)
+            @pl.when(lax.rem(shard, 2) != row)
             def _():
-                keep(lax.rem(shard, half)).start()
-
-            @pl.when(jnp.logical_not(mine))
-            def _():
-                exchange(lax.rem(shard, half)).start()
+                exchange(shard // 2).start()
 
     def forward(step, sub):
         for way in range(2):
@@ -347,10 +395,20 @@
             compute(shard_at(-step), sub)
             compute(shard_at(step), sub)
             forward(step, sub)
+            if sub == 0:
+                adam_block(shard_at(1 - step))
+            if sub == 2:
+
+                @pl.when(step > 1)
+                def _():
+                    adam_block(shard_at(step - 1))
+
 
     for sub in range(subs):
         compute(shard_at(1 - half), sub)
         compute(shard_at(half - 1), sub)
+    adam_block(shard_at(2 - half))
+    adam_block(shard_at(half - 2))
     for sub in range(subs):
         ag_copy(sub // 2, half - 1, sub).wait_recv()
     for sub in range(subs):
@@ -358,6 +416,9 @@
     pre_grad_ref[...] = jnp.where(
         preact[...] > 0, code_grad[...] + l1_weight / total_rows, 0.0
     ).astype(jnp.bfloat16)
+    adam_block(shard_at(1 - half))
+    adam_block(shard_at(half - 1))
+    adam_block(shard_at(half))
 
     @pl.loop(0, n - 1)
     def _(step):
@@ -376,18 +437,18 @@
     @pl.loop(0, half)
     def _(block):
         exchange(block).wait_send()
-        exchange(block).wait_recv()
         keep(block).wait()
 
-    @pl.loop(0, blocks)
-    def _(block):
-        swap_enc(block).wait_send()
+    @pl.loop(0, 2 * blocks)
+    def _(block):
         swap_dec(block).wait_send()
 
     save_centered.wait()
 
 
-def residual_step(enc_weight, dec_weight, enc_bias, dec_bias, activations, total_rows):
+def residual_step(
+    enc_weight, dec_weight, enc_bias, dec_bias, activations, dec_first, dec_second, total_rows
+):
     n = lax.axis_size("lat")
     rows, model = activations.shape
     lats = enc_weight.shape[1]
@@ -401,17 +462,16 @@
         out_shape=(
             jax.ShapeDtypeStruct((rows, lats), bf16),
             jax.ShapeDtypeStruct((lats, model // 2), bf16),
-            jax.ShapeDtypeStruct((lats, model // 2), bf16),
             jax.ShapeDtypeStruct((rows, model), bf16),
         ),
-        in_specs=[whole, whole, vmem, vmem, whole],
-        out_specs=(vmem, whole, whole, whole),
+        in_specs=[whole, whole, vmem, vmem, whole, whole, whole],
+        out_specs=(vmem, whole, whole),
         scratch_shapes=[
             pltpu.VMEM((rows, lats), f32),
             pltpu.VMEM((rows, model), bf16),
             pltpu.VMEM((2, model // 2, lats), bf16),
             pltpu.VMEM((2, model // 2 // blocks, lats), f32),
-            pltpu.VMEM((2, lats // blocks, model // 2), f32),
+            pltpu.VMEM((2, lats // blocks // 2, model // 2), f32),
             pltpu.VMEM((2, lats, model // 2), bf16),
             pltpu.VMEM((rows, width), bf16),
             pltpu.VMEM((n, subs, rows // subs, width), bf16),
@@ -432,17 +492,27 @@
             pltpu.SemaphoreType.DMA((2,)),
             pltpu.SemaphoreType.DMA((blocks,)),
             pltpu.SemaphoreType.DMA((blocks,)),
-            pltpu.SemaphoreType.DMA((blocks,)),
-            pltpu.SemaphoreType.DMA((blocks,)),
+            pltpu.SemaphoreType.DMA((2 * blocks,)),
+            pltpu.SemaphoreType.DMA((2 * blocks,)),
             pltpu.SemaphoreType.DMA((half,)),
+            pltpu.SemaphoreType.DMA((2, half)),
+            pltpu.VMEM((half, lats, width), bf16),
         ],
         compiler_params=pltpu.CompilerParams(
-            collective_id=0, has_side_effects=True, vmem_limit_bytes=60 * 1024 * 1024
+            collective_id=0, has_side_effects=True, vmem_limit_bytes=62 * 1024 * 1024
         ),
         cost_estimate=pl.CostEstimate(
             flops=8 * rows * lats * model, bytes_accessed=30 * 1024 * 1024, transcendentals=0
         ),
-    )(enc_weight, dec_weight, enc_bias.reshape(1, -1), dec_bias.reshape(1, -1), activations)
+    )(
+        enc_weight,
+        dec_weight,
+        enc_bias.reshape(1, -1),
+        dec_bias.reshape(1, -1),
+        activations,
+        dec_first,
+        dec_second,
+    )
 
 
 def on_device(
@@ -460,17 +530,15 @@
     row = lax.axis_index("row")
     part = enc_weight.shape[0]
     swap = [(0, 1), (1, 0)]
-    pre_grad, grad_dec_own, grad_dec_peer, centered = residual_step(
-        enc_weight, dec_weight, enc_bias, dec_bias, activations, total_rows
+    pre_grad, dec_step, centered = residual_step(
+        enc_weight, dec_weight, enc_bias, dec_bias, activations, dec_first, dec_second, total_rows
     )
     centered_own = lax.dynamic_slice_in_dim(centered, row * part, part, 1)
     centered_peer = lax.dynamic_slice_in_dim(centered, (1 - row) * part, part, 1)
     grad_out = rows_product(centered_peer, pre_grad).astype(jnp.bfloat16)
     grad_in = lax.ppermute(grad_out, "row", swap)
-    dec_step = adam_step(
-        grad_dec_own.astype(jnp.float32) + grad_dec_peer.astype(jnp.float32), dec_first, dec_second
-    )
-    grad_enc = rows_product(centered_own, pre_grad) + grad_in.astype(jnp.float32)
+    grad_own = lax.optimization_barrier(rows_product(centered_own, pre_grad))
+    grad_enc = grad_own + grad_in.astype(jnp.float32)
     return (adam_step(grad_enc, enc_first, enc_second), dec_step)
 
 

time: 160 us -> 159 us (level)
  matrix products: 20.1 us -> 13.1 us
  Pallas kernels: 127 us -> 132 us
  other arithmetic: 11.6 us -> 9.43 us
  waiting for transfers between devices: 0.01 us -> 2.09 us
  local copies, waits for them, and re-layouts: 0.02 us -> 2.03 us
    dot_general x2, matrix products: 20.1 us -> 13.1 us  [rows_product(): lax.dot_general(left_rows, right_rows, (((0,), (0,)), ((), ())), preferre...]
    pallas_call x1, Pallas kernels: 127 us -> 132 us  [residual_step(): pl.pallas_call(functools.partial(ring_kernel, n, n <= 8, total_rows), out...]
    convert_element_type x1, other arithmetic: 11.6 us -> 9.43 us  [adam_step(): return (scaled_one / (jnp.sqrt(scaled_two) + adam_eps)).astype(jnp.bfloat16)]
    ppermute x1, waiting for transfers between devices: 0.01 us -> 2.09 us  [on_device(): grad_in = lax.ppermute(grad_out, 'row', swap)]
    unnamed x10 -> x9, local copies, waits for them, and re-layouts: 0.02 us -> 2.03 us
  transfers between devices with their start and end apart: 1 -> 1, of which waited for: 0 -> 1; matrix products, arithmetic and copies ran while one was open for 7% -> 3% of each run, Pallas kernels for 0% -> 0%
where the time goes in v3:
time: 159 us
  Pallas kernels  132 us (83%)
  matrix products  13.1 us (8%)
  other arithmetic  9.43 us (6%)
  waiting for transfers between devices  2.09 us (1%)
  local copies, waits for them, and re-layouts  2.03 us (1%)
    pallas_call x1, Pallas kernels, residual_step(): pl.pallas_call(functools.partial(ring_kernel, n, n <= 8, total_rows), out...  132 us
    dot_general x2, matrix products, rows_product(): lax.dot_general(left_rows, right_rows, (((0,), (0,)), ((), ())), preferre...  13.1 us
    convert_element_type x1, other arithmetic, adam_step(): return (scaled_one / (jnp.sqrt(scaled_two) + adam_eps)).astype(jnp.bfloat16)  9.43 us
  transfers between devices with their start and end apart: 1, of which 1 were waited for; matrix products, arithmetic and copies ran while one was open for 3% of the time, Pallas kernels for 0%

profile of v3, /device:TPU:0, one launch (start us, length us, event | category | flops | bytes accessed | tf_op | source)
XLA Modules:
  0.0 159.0 jit_solution(1556542236345317448)
XLA Ops:
  0.6 131.7 %shard_map.104 = (bf16[640,1024]{1,0:T(8,128)(2,1)}, bf16[1024,2048]{1,0:T(8,128)(2,1)}, bf16[640,4096]{1,0:T(8,128)(2,1)}) custom-call(f32[2048,1024]{1,0:T(8,128)} %enc_ref.1, f32[1024,2048]{1,0:T(8,128)} %dec_ref.1, f32[1,1024]{1,0:T(1,128)} %bitcast.5, f32[1,4096]{1,0:T(1,128)} %bitcast.4, bf16[640,4096]{1,0:T(8,128)(2,1)} %acts_ref.1, ...), custom_call_target="tpu_custom_call" | custom-call | flops 21474836480 | bytes 31457280 | tf_op jit(solution)/shard_map/pallas_call | solution.py:460
  132.3 0.0 copy-start.3
  132.4 7.7 %convolution_convert_fusion = bf16[2048,1024]{1,0:T(8,128)(2,1)} fusion(bf16[640,1024]{1,0:T(8,128)(2,1)} %get-tuple-element.6, bf16[640,4096]{1,0:T(8,128)(2,1)} %get-tuple-element.5, s32[]{:T(128)S(6)} %select_n.7), kind=kOutput, calls=%fused_computation.7 | convolution fusion | flops 2686451712 | bytes 8126468 | tf_op jit(solution)/shard_map/dot_general | solution.py:29
  140.1 0.0 collective-permute-start
  140.1 0.0 copy-done.3
  140.1 0.0 copy-start.1
  140.1 0.0 copy-start.2
  140.1 5.4 %fusion.7 = f32[2048,1024]{1,0:T(8,128)S(1)} fusion(bf16[640,1024]{1,0:T(8,128)(2,1)S(1)} %copy-done.3, bf16[640,4096]{1,0:T(8,128)(2,1)} %get-tuple-element.5, s32[]{:T(128)S(6)} %select_n.6), kind=kOutput, calls=%fused_computation.9 | convolution fusion | flops 2684354560 | bytes 12320772 | tf_op jit(solution)/shard_map/dot_general | solution.py:29
  145.5 0.0 copy-start
  145.5 2.1 %collective-permute-done = bf16[2048,1024]{1,0:T(8,128)(2,1)} collective-permute-done((bf16[2048,1024]{1,0:T(8,128)(2,1)}, bf16[2048,1024]{1,0:T(8,128)(2,1)}, u32[]{:S(2)}, u32[]{:S(2)}) %collective-permute-start) | collective-permute-done | bytes 4194336 | tf_op jit(solution)/shard_map/ppermute | solution.py:539
  147.6 0.0 copy-done.1
  147.6 0.0 copy-done.2
  147.6 9.4 %fusion.5 = bf16[2048,1024]{1,0:T(8,128)(2,1)} fusion(bf16[2048,1024]{1,0:T(8,128)(2,1)S(1)} %copy-done.1, f32[2048,1024]{1,0:T(8,128)S(1)} %fusion.7, bf16[2048,1024]{1,0:T(8,128)(2,1)} %collective-permute-done, bf16[2048,1024]{1,0:T(8,128)(2,1)S(1)} %copy-done.2), kind=kLoop, calls=%fused_computation.6 | loop fusion | flops 31457280 | bytes 25165824 | tf_op jit(solution)/shard_map/convert_element_type | solution.py:25
  157.0 0.0 copy-done
  157.0 2.0 %copy.12 = bf16[1024,2048]{1,0:T(8,128)(2,1)} copy(bf16[1024,2048]{1,0:T(8,128)(2,1)S(1)} %copy-done) | data formatting | bytes 8388608
Async XLA Ops:
  132.3 7.7 %copy-start.3 = (bf16[640,1024]{1,0:T(8,128)(2,1)S(1)}, bf16[640,1024]{1,0:T(8,128)(2,1)}, u32[]{:S(2)}) copy-start(bf16[640,1024]{1,0:T(8,128)(2,1)} %get-tuple-element.6) | copy-start | bytes 3932164
  140.1 7.5 %collective-permute-start = (bf16[2048,1024]{1,0:T(8,128)(2,1)}, bf16[2048,1024]{1,0:T(8,128)(2,1)}, u32[]{:S(2)}, u32[]{:S(2)}) collective-permute-start(bf16[2048,1024]{1,0:T(8,128)(2,1)} %convolution_convert_fusion), channel_id=1, source_target_pairs={{0,1},{1,0},{2,3},{3,2},{4,5},{5,4},{6,7},{7,6},{8,9},{9,8},{10,11... | collective-permute-start | bytes 12582920 | tf_op jit(solution)/shard_map/ppermute | solution.py:539
  140.1 7.5 %copy-start.1 = (bf16[2048,1024]{1,0:T(8,128)(2,1)S(1)}, bf16[2048,1024]{1,0:T(8,128)(2,1)}, u32[]{:S(2)}) copy-start(bf16[2048,1024]{1,0:T(8,128)(2,1)} %param.15) | copy-start | bytes 12582916
  140.1 7.5 %copy-start.2 = (bf16[2048,1024]{1,0:T(8,128)(2,1)S(1)}, bf16[2048,1024]{1,0:T(8,128)(2,1)}, u32[]{:S(2)}) copy-start(bf16[2048,1024]{1,0:T(8,128)(2,1)} %param.14) | copy-start | bytes 12582916
  145.5 11.5 %copy-start = (bf16[1024,2048]{1,0:T(8,128)(2,1)S(1)}, bf16[1024,2048]{1,0:T(8,128)(2,1)}, u32[]{:S(2)}) copy-start(bf16[1024,2048]{1,0:T(8,128)(2,1)} %get-tuple-element.11) | copy-start | bytes 12582916
